TPU v7x, 512 devices: a whole 4x8x8 slice. The times are simulated.
512 devices in a mesh: dp: 8 (over y), feat: 64 (over x, z, core).
Axes of the slice: x: 4, y: 8, z: 8, core: 2. Of those that a mesh axis runs over, the one named last changes fastest.
Arguments:
- features: bfloat16 [8, 16384, 128], P('dp', None, 'feat'), may hold values from -6 to 6
- tile_weights: bfloat16 [8, 1536, 128, 128], P('dp', 'feat'), may hold values from -0.15625 to 0.15625
- tile_rows: int32 [8, 1536], P('dp', 'feat'), may hold values from 0 to 1
- tile_owners: int32 [8, 1536, 1], P('dp', 'feat'), may hold values from 0 to 63; in each aligned block of 24 rows (0 to 23, 24 to 47, ..., all dimensions but the last counted through in order) at most 2 rows name the same one
- tile_blocks: int32 [8, 1536], P('dp', 'feat'), may hold values from 0 to 1
- tile_counts: int32 [8, 64], P('dp', 'feat'), may hold values from 6 to 24, as said below
- cotangent: bfloat16 [8, 16384, 1024], P('dp', 'feat'), may hold values from -0.046875 to 0.046875
- w_self: bfloat16 [128, 1024], replicated, may hold values from -0.5 to 0.5
- w_neigh: bfloat16 [128, 1024], replicated, may hold values from -0.5 to 0.5
- bias: float32 [1024], replicated, may hold values from -4 to 4
Outputs:
- grad_self: float32 [128, 1024], P(None, 'feat')
- grad_neigh: float32 [128, 1024], P(None, 'feat')
- grad_bias: float32 [1024], P('feat')
Inputs may be any that keep to these rules, and one draw needn't show every extreme that they name: `tile_owners`: among the 24 tile slots of one device at most 2 name one owner, a bound that some block of them reaches. `tile_counts`: in every batch some device has all 24 slots live.
All inputs are finite; a program needn't handle non-finite values.
Results may differ from a plain program's by a relative error of at most 0.008.
Values may be sent and summed in bfloat16 or wider, within the bound.
No kernel may reach another device: no remote copies, remote signals or barrier semaphores. Data moves between devices by JAX's collectives and lax.ppermute only.
A program may use at most 64 MiB of HBM per device.

v0:
```python
import jax
import jax.numpy as jnp
from jax import lax
from jax.sharding import PartitionSpec as P


def silu_slope(pre_act):
    sigmoid_z = jax.nn.sigmoid(pre_act)
    return sigmoid_z * (1.0 + pre_act * (1.0 - sigmoid_z))


def local(
    features,
    tile_weights,
    tile_rows,
    tile_owners,
    tile_blocks,
    tile_counts,
    cotangent,
    w_self,
    w_neigh,
    bias,
):
    owned = lax.all_to_all(features, "feat", split_axis=1, concat_axis=2, tiled=True)[0]
    node_rows, feat_width = owned.shape
    slot_count = tile_weights.shape[1]
    tile_side = tile_weights.shape[2]
    row_blocks = node_rows // tile_side
    peer_count = lax.axis_size("feat")
    row_index = tile_rows[0]
    owner_index = tile_owners[0, :, 0]
    block_index = tile_blocks[0]
    live = jnp.arange(slot_count, dtype=jnp.int32) < tile_counts[0, 0]
    whole = lax.all_gather(owned, "feat", axis=0, tiled=True)
    picked = whole.reshape(-1, tile_side, feat_width)[owner_index * row_blocks + block_index]
    products = jnp.einsum(
        "kij,kjf->kif", tile_weights[0], picked, preferred_element_type=jnp.float32
    )
    select = (
        (row_index[None, :] == jnp.arange(row_blocks, dtype=jnp.int32)[:, None]) & live[None, :]
    ).astype(jnp.float32)
    summed = jnp.einsum("rk,kif->rif", select, products, precision=lax.Precision.HIGHEST)
    neighbour = summed.reshape(node_rows, feat_width).astype(jnp.bfloat16)
    pre_act = (
        jnp.dot(owned, w_self, preferred_element_type=jnp.float32)
        + jnp.dot(neighbour, w_neigh, preferred_element_type=jnp.float32)
        + bias
    )
    slope = (cotangent[0].astype(jnp.float32) * silu_slope(pre_act)).astype(jnp.bfloat16)
    grad_s = jnp.einsum("nf,nh->fh", owned, slope, preferred_element_type=jnp.float32)
    grad_n = jnp.einsum("nf,nh->fh", neighbour, slope, preferred_element_type=jnp.float32)
    grad_b = jnp.sum(slope.astype(jnp.float32), axis=0)
    total_s, total_n, total_b = lax.psum((grad_s, grad_n, grad_b), ("dp", "feat"))
    column_count = w_self.shape[1] // peer_count
    start = lax.axis_index("feat") * column_count
    out_s = lax.dynamic_slice_in_dim(total_s, start, column_count, 1)
    out_n = lax.dynamic_slice_in_dim(total_n, start, column_count, 1)
    out_b = lax.dynamic_slice_in_dim(total_b, start, column_count, 0)
    return (out_s, out_n, out_b)


def solution(mesh):
    return jax.shard_map(
        local,
        mesh=mesh,
        in_specs=(
            P("dp", None, "feat"),
            P("dp", "feat", None, None),
            P("dp", "feat"),
            P("dp", "feat", None),
            P("dp", "feat"),
            P("dp", "feat"),
            P("dp", "feat", None),
            P(),
            P(),
            P(),
        ),
        out_specs=(P(None, "feat"), P(None, "feat"), P("feat")),
        check_vma=False,
    )
```

profile of v0, /device:TPU:23, one launch (start us, length us, event | category | flops | bytes accessed | tf_op | source)
XLA Modules:
  0.0 554.2 jit_solution(6314317441695136422)
XLA Ops:
  7.2 15.4 %copy.26 = bf16[1,16384,2]{2,0,1:T(2,128)(2,1)} copy(bf16[1,16384,2]{1,2,0:T(2,128)(2,1)} %param.10) | data formatting | bytes 131072 | tf_op args[0]
  22.6 0.5 broadcast.52
  23.1 90.8 %reduce = bf16[16384,2]{1,0:T(8,128)(2,1)} reduce(bf16[16384,1,2]{2,1,0:T(2,128)(2,1)} %bitcast.51, bf16[]{:T(256)} %broadcast.52), dimensions={1}, to_apply=%bitcast.36.reduce_sub_computation | reduce | bytes 131074
  113.9 7.1 %reshape.61 = bf16[64,2,256]{2,1,0:T(2,128)(2,1)S(1)} reshape(bf16[16384,2]{1,0:T(8,128)(2,1)} %reduce) | data formatting | bytes 131072
  121.0 21.9 %all_to_all.15 = bf16[64,2,256]{2,1,0:T(2,128)(2,1)S(1)} all-to-all(bf16[64,2,256]{2,1,0:T(2,128)(2,1)S(1)} %reshape.61), channel_id=1, replica_groups=mesh['dp'=8,'feat'=64] {'feat'}, dimensions={0} | all-to-all | bytes 131072 | tf_op jit(solution)/shard_map/all_to_all | solution.py:24
  142.9 16.4 %reshape.62 = bf16[16384,1,2]{2,1,0:T(2,128)(2,1)} reshape(bf16[64,2,256]{2,1,0:T(2,128)(2,1)S(1)} %all_to_all.15) | data formatting | bytes 131072
  159.3 15.4 %copy.27 = bf16[1,16384,2]{1,2,0:T(2,128)(2,1)S(1)} copy(bf16[1,16384,2]{2,0,1:T(2,128)(2,1)} %bitcast.52) | data formatting | bytes 131072 | tf_op jit(solution)/shard_map/all_to_all | solution.py:24
  174.7 0.1 copy.28
  174.8 0.7 squeeze.14
  175.5 0.2 all-reduce.3.cloned.1.call-start
  176.4 1.2 fusion.10
  177.6 77.5 %all-gather.2.cloned.1.call-done = bf16[16384,128]{0,1:T(8,128)(2,1)} async-done(((bf16[256,128]{0,1:T(8,128)(2,1)}), bf16[16384,128]{0,1:T(8,128)(2,1)}) %all-gather.2.cloned.1.call-update) | async-done | bytes 4194320 | tf_op jit(solution)/shard_map/all_gather | solution.py:34
  255.0 6.4 %copy.29 = bf16[16384,128]{1,0:T(8,128)(2,1)} copy(bf16[16384,128]{0,1:T(8,128)(2,1)} %all-gather.2.cloned.1.call-done) | data formatting | bytes 8388608 | tf_op jit(solution)/shard_map/all_gather | solution.py:34
  261.4 2.9 gather_fusion
  264.4 1.9 convolution_bitcast_fusion
  266.2 2.0 copy.31
  268.2 0.6 convolution_convert_fusion
  268.9 1.8 convert_reduce_fusion
  270.6 1.1 fusion.11
  271.8 1.1 convolution_bitcast_fusion.1
  272.9 96.3 %psum.23 = f32[1024]{0:T(1024)S(1)} all-reduce(f32[1024]{0:T(1024)S(1)} %get-tuple-element.5), channel_id=1, replica_groups=mesh['dp'=8,'feat'=64] {'dp','feat'}, use_global_device_ids=true, to_apply=%region_3.0 | all-reduce | flops 1024 | bytes 8192 | tf_op jit(solution)/shard_map/psum | solution.py:53
  369.3 0.6 dynamic_slice.11
  369.9 176.2 %all-reduce.3.cloned.1.call-done = (f32[128,1024]{0,1:T(8,128)}, f32[128,1024]{0,1:T(8,128)}) async-done(((f32[128,1024]{0,1:T(8,128)}, f32[128,1024]{0,1:T(8,128)}), (f32[128,1024]{0,1:T(8,128)}, f32[128,1024]{0,1:T(8,128)})) %all-reduce.3.cloned.1.call-update) | async-done | bytes 1048592 | tf_op jit(solution)/shard_map/psum | solution.py:53
  546.0 1.3 constant_dynamic-slice_fusion
  (22 shorter events, 0.1 us)
Async XLA Ops:
  7.2 257.2 %copy-start = (bf16[1,24,128,128]{3,2,1,0:T(8,128)(2,1)S(1)}, bf16[1,24,128,128]{3,2,1,0:T(8,128)(2,1)}, u32[]{:S(2)}) copy-start(bf16[1,24,128,128]{3,2,1,0:T(8,128)(2,1)} %param.11) | copy-start | bytes 2359300
  7.2 247.8 %all-gather.2.cloned.1.call-start = ((), (), s32[]{:S(2)}) async-start(), calls=%async_computation.1 | async-start | bytes 4259840 | tf_op jit(solution)/shard_map/all_gather | solution.py:34
  159.3 17.1 %copy-start.5 = (s32[1,24]{1,0:T(1,128)S(1)}, s32[1,24]{1,0:T(1,128)}, u32[]{:S(2)}) copy-start(s32[1,24]{1,0:T(1,128)} %param.14) | copy-start | bytes 292
  159.3 17.1 %copy-start.6 = (s32[1,24,1]{1,2,0:T(1,128)S(1)}, s32[1,24,1]{1,2,0:T(1,128)}, u32[]{:S(2)}) copy-start(s32[1,24,1]{1,2,0:T(1,128)} %param.13) | copy-start | bytes 292
  159.3 17.1 %copy-start.2 = (bf16[128,1024]{1,0:T(8,128)(2,1)S(1)}, bf16[128,1024]{1,0:T(8,128)(2,1)}, u32[]{:S(2)}) copy-start(bf16[128,1024]{1,0:T(8,128)(2,1)} %param.17) | copy-start | bytes 786436
  175.5 370.6 %all-reduce.3.cloned.1.call-start = ((), (), s32[]{:S(2)}) async-start(), calls=%async_computation.2 | async-start | bytes 2097152 | tf_op jit(solution)/shard_map/psum | solution.py:53
  261.4 6.8 %copy-start.3 = (s32[1,24]{1,0:T(1,128)S(1)}, s32[1,24]{1,0:T(1,128)}, u32[]{:S(2)}) copy-start(s32[1,24]{1,0:T(1,128)} %param.12) | copy-start | bytes 292
  264.4 4.5 copy-start.4
  268.8 3.0 copy-start.1
Sparse Core Ops, SparseCore 0:
  175.6 79.3 all-gather.1
  273.1 272.9 all-reduce.2
where the time goes:
time: 556 us; the launch traced here: 554 us
  waiting for transfers between devices  254 us (46%)
  blocking collectives  118 us (21%)
  other arithmetic  90.8 us (16%)
  local copies, waits for them, and re-layouts  68.7 us (12%)
  between operations  14.9 us (3%)
  matrix products  7.67 us (1%)
    psum x1, waiting for transfers between devices, local(): lax.psum((grad_s, grad_n, grad_b), ('dp', 'feat'))  176 us
    psum x1, blocking collectives, local(): lax.psum((grad_s, grad_n, grad_b), ('dp', 'feat'))  96.3 us
    unnamed x1, other arithmetic  90.8 us
    all_gather x1, waiting for transfers between devices, local(): whole = lax.all_gather(owned, 'feat', axis=0, tiled=True)  77.5 us
    unnamed x19, local copies, waits for them, and re-layouts  39.5 us
    all_to_all x1, blocking collectives, local(): lax.all_to_all(features, 'feat', split_axis=1, concat_axis=2, tiled=True)[0]  21.9 us
    all_to_all x2, local copies, waits for them, and re-layouts, local(): lax.all_to_all(features, 'feat', split_axis=1, concat_axis=2, tiled=True)[0]  15.5 us
  transfers between devices with their start and end apart: 2, of which 2 were waited for; matrix products, arithmetic and copies ran while one was open for 0% of the time, Pallas kernels for 0%

commit v1 on v0

--- a/solution.py
+++ b/solution.py
@@ -31,7 +31,15 @@
     owner_index = tile_owners[0, :, 0]
     block_index = tile_blocks[0]
     live = jnp.arange(slot_count, dtype=jnp.int32) < tile_counts[0, 0]
-    whole = lax.all_gather(owned, "feat", axis=0, tiled=True)
+    ways, here = (lax.axis_size("feat"), lax.axis_index("feat"))
+    grown, reach = (owned, 1)
+    while reach < ways:
+        theirs = lax.ppermute(grown, "feat", [(d, d ^ reach) for d in range(ways)])
+        mine_first = jnp.concatenate([grown, theirs], axis=0)
+        theirs_first = jnp.concatenate([theirs, grown], axis=0)
+        grown = jnp.where(here & reach == 0, mine_first, theirs_first)
+        reach = 2 * reach
+    whole = grown
     picked = whole.reshape(-1, tile_side, feat_width)[owner_index * row_blocks + block_index]
     products = jnp.einsum(
         "kij,kjf->kif", tile_weights[0], picked, preferred_element_type=jnp.float32

time: 556 us -> 615 us (1.11)
  waiting for transfers between devices: 254 us -> 283 us
  starting transfers between devices: 0.26 us -> 15.9 us
  other arithmetic: 90.8 us -> 98.5 us
  blocking collectives: 118 us -> 125 us
    ppermute x0 -> x6, waiting for transfers between devices: none -> 109 us  [local(): theirs = lax.ppermute(grown, 'feat', [(d, d ^ reach) for d in range(ways)])]
    all_gather x1 -> x0, waiting for transfers between devices: 77.5 us -> none  [local(): whole = lax.all_gather(owned, 'feat', axis=0, tiled=True)]
    ppermute x0 -> x6, starting transfers between devices: none -> 15.9 us  [local(): theirs = lax.ppermute(grown, 'feat', [(d, d ^ reach) for d in range(ways)])]
    select_n x0 -> x6, other arithmetic: none -> 7.73 us  [local(): grown = jnp.where(here & reach == 0, mine_first, theirs_first)]
    psum x1, blocking collectives: 96.3 us -> 103 us  [local(): lax.psum((grad_s, grad_n, grad_b), ('dp', 'feat'))]
    all_gather x1 -> x0, local copies, waits for them, and re-layouts: 6.42 us -> none  [local(): whole = lax.all_gather(owned, 'feat', axis=0, tiled=True)]
    select_n x0 -> x1, local copies, waits for them, and re-layouts: none -> 6.41 us  [local(): grown = jnp.where(here & reach == 0, mine_first, theirs_first)]
    unnamed x19 -> x21, local copies, waits for them, and re-layouts: 39.5 us -> 39.5 us
  transfers between devices with their start and end apart: 2 -> 7, of which waited for: 2 -> 7; matrix products, arithmetic and copies ran while one was open for 0% -> 0% of each run, Pallas kernels for 0% -> 0%
where the time goes in v1:
time: 615 us; the launch traced here: 613 us
  waiting for transfers between devices  283 us (46%)
  blocking collectives  125 us (20%)
  other arithmetic  98.5 us (16%)
  local copies, waits for them, and re-layouts  68.1 us (11%)
  starting transfers between devices  15.9 us (3%)
  between operations  15 us (2%)
  matrix products  7.91 us (1%)
    psum x1, waiting for transfers between devices, local(): lax.psum((grad_s, grad_n, grad_b), ('dp', 'feat'))  175 us
    ppermute x6, waiting for transfers between devices, local(): theirs = lax.ppermute(grown, 'feat', [(d, d ^ reach) for d in range(ways)])  109 us
    psum x1, blocking collectives, local(): lax.psum((grad_s, grad_n, grad_b), ('dp', 'feat'))  103 us
    unnamed x1, other arithmetic  90.8 us
    unnamed x21, local copies, waits for them, and re-layouts  39.5 us
    all_to_all x1, blocking collectives, local(): lax.all_to_all(features, 'feat', split_axis=1, concat_axis=2, tiled=True)[0]  21.9 us
    ppermute x6, starting transfers between devices, local(): theirs = lax.ppermute(grown, 'feat', [(d, d ^ reach) for d in range(ways)])  15.9 us
    all_to_all x2, local copies, waits for them, and re-layouts, local(): lax.all_to_all(features, 'feat', split_axis=1, concat_axis=2, tiled=True)[0]  15.4 us
  transfers between devices with their start and end apart: 7, of which 7 were waited for; matrix products, arithmetic and copies ran while one was open for 0% of the time, Pallas kernels for 0%

profile of v1, /device:TPU:23, one launch (start us, length us, event | category | flops | bytes accessed | tf_op | source)
XLA Modules:
  0.0 613.3 jit_solution(4694558539701994349)
XLA Ops:
  7.2 15.3 %copy.26 = bf16[1,16384,2]{2,0,1:T(2,128)(2,1)} copy(bf16[1,16384,2]{1,2,0:T(2,128)(2,1)} %param.10) | data formatting | bytes 131072 | tf_op args[0]
  23.1 90.8 %reduce = bf16[16384,2]{1,0:T(8,128)(2,1)} reduce(bf16[16384,1,2]{2,1,0:T(2,128)(2,1)} %bitcast.51, bf16[]{:T(256)} %broadcast.55), dimensions={1}, to_apply=%bitcast.36.reduce_sub_computation | reduce | bytes 131074
  113.8 7.1 %reshape.62 = bf16[64,2,256]{2,1,0:T(2,128)(2,1)S(1)} reshape(bf16[16384,2]{1,0:T(8,128)(2,1)} %reduce) | data formatting | bytes 131072
  121.0 21.9 %all_to_all.15 = bf16[64,2,256]{2,1,0:T(2,128)(2,1)S(1)} all-to-all(bf16[64,2,256]{2,1,0:T(2,128)(2,1)S(1)} %reshape.62), channel_id=1, replica_groups=mesh['dp'=8,'feat'=64] {'feat'}, dimensions={0} | all-to-all | bytes 131072 | tf_op jit(solution)/shard_map/all_to_all | solution.py:24
  142.9 16.4 %reshape.63 = bf16[16384,1,2]{2,1,0:T(2,128)(2,1)} reshape(bf16[64,2,256]{2,1,0:T(2,128)(2,1)S(1)} %all_to_all.15) | data formatting | bytes 131072
  159.3 15.3 %copy.27 = bf16[1,16384,2]{1,2,0:T(2,128)(2,1)S(1)} copy(bf16[1,16384,2]{2,0,1:T(2,128)(2,1)} %bitcast.52) | data formatting | bytes 131072 | tf_op jit(solution)/shard_map/all_to_all | solution.py:24
  174.8 2.3 collective-permute-start
  178.0 2.4 collective-permute-start.1
  180.5 4.2 collective-permute-done.1
  184.7 2.6 collective-permute-start.2
  187.3 13.8 %collective-permute-done.2 = bf16[1024,128]{0,1:T(8,128)(2,1)S(1)} collective-permute-done((bf16[1024,128]{0,1:T(8,128)(2,1)S(1)}, bf16[1024,128]{0,1:T(8,128)(2,1)S(1)}, u32[]{:S(2)}, u32[]{:S(2)}) %collective-permute-start.2) | collective-permute-done | bytes 262176 | tf_op jit(solution)/shard_map/ppermute | solution.py:37
  201.3 2.2 collective-permute-start.3
  203.5 25.0 %collective-permute-done.3 = bf16[2048,128]{0,1:T(8,128)(2,1)S(1)} collective-permute-done((bf16[2048,128]{0,1:T(8,128)(2,1)S(1)}, bf16[2048,128]{0,1:T(8,128)(2,1)S(1)}, u32[]{:S(2)}, u32[]{:S(2)}) %collective-permute-start.3) | collective-permute-done | bytes 524320 | tf_op jit(solution)/shard_map/ppermute | solution.py:37
  228.7 2.2 collective-permute-start.4
  231.0 22.8 %collective-permute-done.4 = bf16[4096,128]{0,1:T(8,128)(2,1)} collective-permute-done((bf16[4096,128]{0,1:T(8,128)(2,1)S(1)}, bf16[4096,128]{0,1:T(8,128)(2,1)}, u32[]{:S(2)}, u32[]{:S(2)}) %collective-permute-start.4) | collective-permute-done | bytes 1048608 | tf_op jit(solution)/shard_map/ppermute | solution.py:37
  253.8 2.7 maximum_select_fusion.1
  256.5 4.1 collective-permute-start.5
  262.7 41.9 %collective-permute-done.5 = bf16[8192,128]{0,1:T(8,128)(2,1)} collective-permute-done((bf16[8192,128]{0,1:T(8,128)(2,1)S(1)}, bf16[8192,128]{0,1:T(8,128)(2,1)}, u32[]{:S(2)}, u32[]{:S(2)}) %collective-permute-start.5) | collective-permute-done | bytes 2097184 | tf_op jit(solution)/shard_map/ppermute | solution.py:37
  304.6 4.5 maximum_select_fusion
  309.1 6.4 %copy.29 = bf16[16384,128]{1,0:T(8,128)(2,1)} copy(bf16[16384,128]{0,1:T(8,128)(2,1)} %maximum_select_fusion) | data formatting | bytes 8388608 | tf_op jit(solution)/shard_map/jit(_where)/select_n | solution.py:40
  315.5 2.9 gather_fusion
  320.3 2.0 copy.31
  327.1 103.0 %psum.23 = f32[1024]{0:T(1024)S(1)} all-reduce(f32[1024]{0:T(1024)S(1)} %get-tuple-element.5), channel_id=1, replica_groups=mesh['dp'=8,'feat'=64] {'dp','feat'}, use_global_device_ids=true, to_apply=%region_3.4 | all-reduce | flops 1024 | bytes 8192 | tf_op jit(solution)/shard_map/psum | solution.py:61
  430.6 174.5 %all-reduce.3.cloned.1.call-done = (f32[128,1024]{0,1:T(8,128)}, f32[128,1024]{0,1:T(8,128)}) async-done(((f32[128,1024]{0,1:T(8,128)}, f32[128,1024]{0,1:T(8,128)}), (f32[128,1024]{0,1:T(8,128)}, f32[128,1024]{0,1:T(8,128)})) %all-reduce.3.cloned.1.call-update) | async-done | bytes 1048592 | tf_op jit(solution)/shard_map/psum | solution.py:61
  (39 shorter events, 11.9 us)
Async XLA Ops:
  7.2 311.3 %copy-start = (bf16[1,24,128,128]{3,2,1,0:T(8,128)(2,1)S(1)}, bf16[1,24,128,128]{3,2,1,0:T(8,128)(2,1)}, u32[]{:S(2)}) copy-start(bf16[1,24,128,128]{3,2,1,0:T(8,128)(2,1)} %param.11) | copy-start | bytes 2359300
  7.2 598.0 %all-reduce.3.cloned.1.call-start = ((), (), s32[]{:S(2)}) async-start(), calls=%async_computation.1 | async-start | bytes 2097152 | tf_op jit(solution)/shard_map/psum | solution.py:61
  174.6 86.6 %copy-start.6 = (s32[1,24]{1,0:T(1,128)S(1)}, s32[1,24]{1,0:T(1,128)}, u32[]{:S(2)}) copy-start(s32[1,24]{1,0:T(1,128)} %param.14) | copy-start | bytes 292
  174.7 86.6 %copy-start.7 = (s32[1,24,1]{1,2,0:T(1,128)S(1)}, s32[1,24,1]{1,2,0:T(1,128)}, u32[]{:S(2)}) copy-start(s32[1,24,1]{1,2,0:T(1,128)} %param.13) | copy-start | bytes 292
  174.7 86.7 %copy-start.3 = (bf16[128,1024]{1,0:T(8,128)(2,1)S(1)}, bf16[128,1024]{1,0:T(8,128)(2,1)}, u32[]{:S(2)}) copy-start(bf16[128,1024]{1,0:T(8,128)(2,1)} %param.17) | copy-start | bytes 786436
  174.8 3.2 collective-permute-start
  178.0 6.6 %collective-permute-start.1 = (bf16[512,128]{0,1:T(8,128)(2,1)S(1)}, bf16[512,128]{0,1:T(8,128)(2,1)S(1)}, u32[]{:S(2)}, u32[]{:S(2)}) collective-permute-start(bf16[512,128]{0,1:T(8,128)(2,1)S(1)} %maximum_select_fusion.5), channel_id=1, source_target_pairs={{0,2},{1,3},{2,0},{3,1},{4,6},{5,7},{6,4},{7,5},{8,10},{9,11},{10,... | collective-permute-start | bytes 393224 | tf_op jit(solution)/shard_map/ppermute | solution.py:37
  184.7 16.4 %collective-permute-start.2 = (bf16[1024,128]{0,1:T(8,128)(2,1)S(1)}, bf16[1024,128]{0,1:T(8,128)(2,1)S(1)}, u32[]{:S(2)}, u32[]{:S(2)}) collective-permute-start(bf16[1024,128]{0,1:T(8,128)(2,1)S(1)} %maximum_select_fusion.4), channel_id=1, source_target_pairs={{0,4},{1,5},{2,6},{3,7},{4,0},{5,1},{6,2},{7,3},{8,12},{9,13},{10,... | collective-permute-start | bytes 786440 | tf_op jit(solution)/shard_map/ppermute | solution.py:37
  201.3 27.1 %collective-permute-start.3 = (bf16[2048,128]{0,1:T(8,128)(2,1)S(1)}, bf16[2048,128]{0,1:T(8,128)(2,1)S(1)}, u32[]{:S(2)}, u32[]{:S(2)}) collective-permute-start(bf16[2048,128]{0,1:T(8,128)(2,1)S(1)} %maximum_select_fusion.3), channel_id=1, source_target_pairs={{0,8},{1,9},{2,10},{3,11},{4,12},{5,13},{6,14},{7,15},{8,0},{9,1},... | collective-permute-start | bytes 1572872 | tf_op jit(solution)/shard_map/ppermute | solution.py:37
  228.7 2.3 copy-start.1
  228.7 25.1 %collective-permute-start.4 = (bf16[4096,128]{0,1:T(8,128)(2,1)S(1)}, bf16[4096,128]{0,1:T(8,128)(2,1)}, u32[]{:S(2)}, u32[]{:S(2)}) collective-permute-start(bf16[4096,128]{0,1:T(8,128)(2,1)S(1)} %maximum_select_fusion.2), channel_id=1, source_target_pairs={{0,16},{1,17},{2,18},{3,19},{4,20},{5,21},{6,22},{7,23},{8,24},{9,... | collective-permute-start | bytes 3145736 | tf_op jit(solution)/shard_map/ppermute | solution.py:37
  256.5 48.1 %collective-permute-start.5 = (bf16[8192,128]{0,1:T(8,128)(2,1)S(1)}, bf16[8192,128]{0,1:T(8,128)(2,1)}, u32[]{:S(2)}, u32[]{:S(2)}) collective-permute-start(bf16[8192,128]{0,1:T(8,128)(2,1)S(1)} %maximum_select_fusion.1), channel_id=1, source_target_pairs={{0,32},{1,33},{2,34},{3,35},{4,36},{5,37},{6,38},{7,39},{8,40},{9,... | collective-permute-start | bytes 6291464 | tf_op jit(solution)/shard_map/ppermute | solution.py:37
  315.5 6.7 %copy-start.4 = (s32[1,24]{1,0:T(1,128)S(1)}, s32[1,24]{1,0:T(1,128)}, u32[]{:S(2)}) copy-start(s32[1,24]{1,0:T(1,128)} %param.12) | copy-start | bytes 292
  318.4 4.5 copy-start.2
  318.5 4.5 copy-start.5
Sparse Core Ops, SparseCore 0:
  327.2 277.9 all-reduce.2
